TPU v7x, 32 devices: a whole 2x2x4 slice. The times are simulated.
32 devices in a mesh: groups: 2 (over y), row: 4 (over z), col: 2 (over x), pole: 2 (over core).
Axes of the slice: x: 2, y: 2, z: 4, core: 2. Of those that a mesh axis runs over, the one named last changes fastest.
Arguments:
- inverse: bfloat16 [4, 2, 8192, 8192], P(('groups', 'pole'), None, 'row', 'col'), parts along dimension 0, may hold values from -6 to 6
- lower: bfloat16 [4, 8192, 2, 3, 256], P(('groups', 'pole'), ('col', 'row')), parts along dimension 0, may hold values from -0.0625 to 0.0625
- upper: bfloat16 [4, 8192, 2, 3, 256], P(('groups', 'pole'), ('row', 'col')), parts along dimension 0, may hold values from -0.0625 to 0.0625
- diag_inverse: bfloat16 [4, 3, 2, 256, 256], P(('groups', 'pole')), parts along dimension 0, may hold values from -6 to 6
- weights: float32 [4, 2], P(('groups', 'pole')), parts along dimension 0, may hold values from -4 to 4
- pattern: int32 [6, 16], P('groups'), parts along dimension 0, may hold values from 0 to 31, as said below
Outputs:
- column_density: float32 [16384, 3, 256], P(('groups', 'row', 'col', 'pole')), parts along dimension 0
- row_density: float32 [16384, 3, 256], P(('groups', 'col', 'row', 'pole')), parts along dimension 0
- diagonal_density: float32 [6, 256, 256], P('groups'), parts along dimension 0
There are 2 independent parts, one for each index of `groups`. A program takes and returns all parts, laid end to end along the dimension named above; each array names one. Nothing has to cross between parts.
Inputs may be any that keep to these rules, and one draw needn't show every extreme that they name: `pattern`: each row names 16 different ancestor blocks, and the rows together name every ancestor block.
All inputs are finite; a program needn't handle non-finite values.
Results may differ from a plain program's by a relative error of at most 0.0003.
Values may be sent and summed in bfloat16 or wider, within the bound.
No kernel may reach another device: no remote copies, remote signals or barrier semaphores. Data moves between devices by JAX's collectives and lax.ppermute only.
A program may use at most 192 MiB of HBM per device.

v0:
```python
import jax
import jax.numpy as jnp
from jax import lax
from jax.sharding import PartitionSpec as P


def masked(factor, pattern, start):
    count = factor.shape[0]
    width = factor.shape[3]
    blocks = (start + lax.iota(jnp.int32, count)) // width
    hits = pattern[:, :, None] == blocks[None, None, :]
    keep = jnp.transpose(jnp.any(hits, axis=1))[:, None, :, None]
    return jnp.where(keep, factor, jnp.zeros_like(factor))


def paired(factor):
    count = factor.shape[0]
    flat = factor.reshape(count, 2, -1)
    real_part = flat[:, 0]
    imag_part = flat[:, 1]
    upper_half = jnp.concatenate([real_part, imag_part], axis=1)
    lower_half = jnp.concatenate([-imag_part, real_part], axis=1)
    return (upper_half, lower_half)


def weighted(values, weight_real, weight_imag):
    half = values.shape[1] // 2
    return weight_real * values[:, half:] + weight_imag * values[:, :half]


def diagonal_term(terms, piece, weight_real, weight_imag):
    count = piece.shape[0]
    supernodes = piece.shape[2]
    width = piece.shape[3]
    half = supernodes * width
    real_terms = terms[:, :half].reshape(count, supernodes, width).astype(jnp.float32)
    imag_terms = terms[:, half:].reshape(count, supernodes, width).astype(jnp.float32)
    real_piece = piece[:, 0]
    imag_piece = piece[:, 1]
    first_mix = weight_real * imag_piece + weight_imag * real_piece
    second_mix = weight_real * real_piece - weight_imag * imag_piece
    highest = lax.Precision.HIGHEST
    return jnp.einsum("nsa,nsb->sab", real_terms, first_mix, precision=highest) + jnp.einsum(
        "nsa,nsb->sab", imag_terms, second_mix, precision=highest
    )


def body(inverse, lower, upper, diag_inverse, weights, pattern):
    n_row = lax.axis_size("row")
    n_col = lax.axis_size("col")
    row_index = lax.axis_index("row")
    col_index = lax.axis_index("col")
    local_rows = lower.shape[1]
    supernodes = lower.shape[3]
    width = lower.shape[4]
    half = supernodes * width
    real_inverse = inverse[0, 0]
    imag_inverse = inverse[0, 1]
    part_rows = real_inverse.shape[0]
    part_cols = real_inverse.shape[1]
    weight_real = weights[0, 0]
    weight_imag = weights[0, 1]
    lower_kept = masked(lower[0], pattern, (col_index * n_row + row_index) * local_rows)
    upper_kept = masked(upper[0], pattern, (row_index * n_col + col_index) * local_rows)
    upper_rows = lax.all_gather(upper_kept, "col", axis=0, tiled=True)
    upper_first, upper_second = paired(upper_rows)
    stacked_upper = jnp.concatenate([upper_first, upper_second], axis=0)
    stacked_inverse = inverse[0].reshape(2 * part_rows, part_cols)
    first_part, second_part = paired(lax.all_gather(lower_kept, "row", axis=0, tiled=True))
    product = jnp.dot(real_inverse, first_part, preferred_element_type=jnp.float32) + jnp.dot(
        imag_inverse, second_part, preferred_element_type=jnp.float32
    )
    column_part = -weighted(product, weight_real, weight_imag)
    column_density = lax.psum_scatter(
        column_part.reshape(part_rows, supernodes, width),
        ("col", "pole"),
        scatter_dimension=0,
        tiled=True,
    )
    transposed_terms = lax.dot_general(
        stacked_inverse, stacked_upper, (((0,), (0,)), ((), ())), preferred_element_type=jnp.float32
    )
    upper_flat = upper_rows.reshape(part_rows, 2 * half)
    product_piece = product.reshape(part_rows, 2, supernodes, width)
    diag_part = diagonal_term(upper_flat, product_piece, weight_real, weight_imag)
    row_part = -weighted(transposed_terms, weight_real, weight_imag)
    row_density = lax.psum_scatter(
        row_part.reshape(part_cols, supernodes, width),
        ("row", "pole"),
        scatter_dimension=0,
        tiled=True,
    )
    first_device = jnp.logical_and(row_index == 0, col_index == 0)
    given = diag_inverse[0].astype(jnp.float32)
    own_term = weight_real * given[:, 1] + weight_imag * given[:, 0]
    diag_part = diag_part + jnp.where(first_device, own_term, jnp.zeros_like(own_term))
    diagonal_density = lax.psum(diag_part, ("row", "col", "pole"))
    return (column_density, row_density, diagonal_density)


def solution(mesh):
    return jax.shard_map(
        body,
        mesh=mesh,
        in_specs=(
            P(("groups", "pole"), None, "row", "col"),
            P(("groups", "pole"), ("col", "row"), None, None, None),
            P(("groups", "pole"), ("row", "col"), None, None, None),
            P(("groups", "pole"), None, None, None, None),
            P(("groups", "pole"), None),
            P("groups", None),
        ),
        out_specs=(
            P(("groups", "row", "col", "pole"), None, None),
            P(("groups", "col", "row", "pole"), None, None),
            P("groups", None, None),
        ),
        check_vma=False,
    )
```

profile of v0, /device:TPU:0, one launch (start us, length us, event | category | flops | bytes accessed | tf_op | source)
XLA Modules:
  0.0 738.2 jit_solution(1963326459483459146)
XLA Ops:
  7.2 7.0 copy.43
  16.4 7.0 copy.38
  26.1 2.5 bitcast_convert_fusion
  28.6 71.0 %all-gather.5.cloned.1.call-done = bf16[2048,2,3,256]{0,3,2,1:T(8,128)(2,1)} async-done(((bf16[1024,2,3,256]{0,3,2,1:T(8,128)(2,1)}), bf16[2048,2,3,256]{0,3,2,1:T(8,128)(2,1)}) %all-gather.5.cloned.1.call-update) | async-done | bytes 6291472 | tf_op jit(solution)/shard_map/all_gather | solution.py:65
  99.6 4.0 fusion.60
  104.5 3.4 slice_bitcast_fusion.2
  107.8 3.8 fusion.63
  111.6 207.8 %all-gather.3.cloned.1.call-done = bf16[4096,2,3,256]{0,3,2,1:T(8,128)(2,1)} async-done(((bf16[1024,2,3,256]{0,3,2,1:T(8,128)(2,1)}), bf16[4096,2,3,256]{0,3,2,1:T(8,128)(2,1)}) %all-gather.3.cloned.1.call-update) | async-done | bytes 12582928 | tf_op jit(solution)/shard_map/all_gather | solution.py:69
  319.4 6.5 fusion.61
  328.1 4.8 slice_bitcast_fusion
  332.8 34.6 %fusion = f32[1536,2048]{1,0:T(8,128)} fusion(bf16[1,2,2048,4096]{3,2,1,0:T(8,128)(2,1)} %param.6, bf16[4096,768]{0,1:T(8,128)(2,1)} %get-tuple-element.8, bf16[4096,768]{0,1:T(8,128)(2,1)} %fusion.61), kind=kOutput, calls=%fused_computation.1 | convolution fusion | flops 25794969600 | bytes 41943040 | tf_op jit(solution)/shard_map/dot_general | solution.py:70
  367.5 35.7 %fusion.21 = f32[1536,2048]{1,0:T(8,128)} fusion(f32[1536,2048]{1,0:T(8,128)} %fusion, bf16[1,2,2048,4096]{3,2,1,0:T(8,128)(2,1)} %param.6, bf16[4096,768]{0,1:T(8,128)(2,1)} %get-tuple-element.7, bf16[4096,768]{0,1:T(8,128)(2,1)} %get-tuple-element.8), kind=kOutput, calls=%fused_computation.24 | convolution fusion | flops 25798115328 | bytes 54525952 | tf_op jit(solution)/shard_map/dot_general | solution.py:70
  403.2 11.3 %fusion.62 = (f32[2048,1,3,256]{0,3,2,1:T(8,128)}, f32[2048,1,3,256]{0,3,2,1:T(8,128)}) fusion(f32[2048,2,3,256]{0,3,2,1:T(8,128)} %bitcast.69), kind=kLoop, calls=%fused_computation.82 | loop fusion | bytes 25165824 | tf_op jit(solution)/shard_map/slice | solution.py:38
  414.5 6.6 copy.56
  421.1 6.9 copy.55
  428.0 12.0 %fusion.28 = f32[3,256,256]{2,1,0:T(8,128)S(1)} fusion(bf16[2048,3,256]{0,2,1:T(8,128)(2,1)} %bitcast.78, f32[2048,1,3,256]{3,0,2,1:T(8,128)} %copy.55, f32[2048,1,3,256]{3,0,2,1:T(8,128)} %copy.56, f32[]{:T(128)} %bitcast.11, f32[]{:T(128)} %bitcast), kind=kOutput, calls=%fused_computation.31 | convolution fusion | flops 4836556800 | bytes 16515080 | tf_op jit(solution)/shard_map/nsa,nsb->sab/dot_general | solution.py:43
  440.1 6.2 fusion.45
  446.4 10.8 %fusion.27 = f32[2048,768]{0,1:T(8,128)} fusion(f32[2048,1536]{0,1:T(8,128)} %bitcast.70, f32[]{:T(128)} %bitcast.11, f32[]{:T(128)} %bitcast), kind=kLoop, calls=%fused_computation.27 | loop fusion | flops 6291456 | bytes 18874376 | tf_op jit(solution)/shard_map/neg | solution.py:73
  457.2 6.6 copy.42
  465.7 84.0 %convolution_bitcast_fusion = f32[4096,1536]{0,1:T(8,128)} fusion(bf16[4096,4096]{1,0:T(8,128)(2,1)} %bitcast.82, bf16[2048,768]{0,1:T(8,128)(2,1)} %get-tuple-element.12, bf16[2048,768]{0,1:T(8,128)(2,1)S(1)} %copy-done.5, bf16[2048,768]{0,1:T(8,128)(2,1)} %get-tuple-element.11), kind=kOutput, calls=%fused_computation | convolution fusion | flops 51589939200 | bytes 68157440 | tf_op jit(solution)/shard_map/dot_general | solution.py:80
  549.7 16.3 %fusion.7 = f32[4096,768]{0,1:T(8,128)} fusion(f32[4096,1536]{0,1:T(8,128)} %convolution_bitcast_fusion, f32[]{:T(128)} %bitcast.11, f32[]{:T(128)} %bitcast), kind=kLoop, calls=%fused_computation.9 | loop fusion | flops 12582912 | bytes 37748744 | tf_op jit(solution)/shard_map/neg | solution.py:86
  566.0 12.6 %copy.47 = f32[4096,3,256]{2,0,1:T(8,128)} copy(f32[4096,3,256]{0,2,1:T(8,128)} %bitcast.71) | data formatting | bytes 25165824 | tf_op jit(solution)/shard_map/reshape | solution.py:88
  578.6 18.5 %reduce-scatter.3.cloned.1.call-done = f32[512,3,256]{2,0,1:T(8,128)} async-done(((f32[2048,3,256]{2,0,1:T(8,128)}), f32[512,3,256]{2,0,1:T(8,128)}) %reduce-scatter.3.cloned.1.call-update) | async-done | bytes 1572880 | tf_op jit(solution)/shard_map/reduce_scatter | solution.py:74
  597.2 132.0 %reduce-scatter.5.cloned.1.call-done = f32[512,3,256]{2,0,1:T(8,128)} async-done(((f32[4096,3,256]{2,0,1:T(8,128)}), f32[512,3,256]{2,0,1:T(8,128)}) %reduce-scatter.5.cloned.1.call-update) | async-done | bytes 1572880 | tf_op jit(solution)/shard_map/reduce_scatter | solution.py:87
  (38 shorter events, 11.8 us)
Async XLA Ops:
  7.2 7.1 copy-start.6
  7.2 92.4 %all-gather.5.cloned.1.call-start = ((), (), s32[]{:S(2)}) async-start(), calls=%async_computation.4 | async-start | bytes 9437184 | tf_op jit(solution)/shard_map/all_gather | solution.py:65
  16.4 303.0 %all-gather.3.cloned.1.call-start = ((), (), s32[]{:S(2)}) async-start(), calls=%async_computation.2 | async-start | bytes 15728640 | tf_op jit(solution)/shard_map/all_gather | solution.py:69
  23.5 2.0 copy-start.7
  25.4 553.2 %all-reduce.2.cloned.1.call-start = ((), (), s32[]{:S(2)}) async-start(), calls=%async_computation.6 | async-start | bytes 1572864 | tf_op jit(solution)/shard_map/psum | solution.py:97
  99.6 4.9 copy-start.1
  319.4 8.7 %copy-start.2 = (bf16[4096,2,3,256]{0,3,2,1:T(8,128)(2,1)S(1)}, bf16[4096,2,3,256]{0,3,2,1:T(8,128)(2,1)}, u32[]{:S(2)}) copy-start(bf16[4096,2,3,256]{0,3,2,1:T(8,128)(2,1)} %all-gather.3.cloned.1.call-done) | copy-start | bytes 37748740
  421.0 19.0 %slice-start = ((s8[6291456]{0:T(1024)(128)(4,1)}), s8[2097152]{0:T(1024)(128)(4,1)S(1)}, s32[]{:S(2)}) async-start(s8[6291456]{0:T(1024)(128)(4,1)} %bitcast.67), calls=%async_computation.7 | async-start | bytes 4194304
  427.9 12.1 %slice-start.1 = ((s8[6291456]{0:T(1024)(128)(4,1)}), s8[4194304]{0:T(1024)(128)(4,1)S(1)}, s32[]{:S(2)}) async-start(s8[6291456]{0:T(1024)(128)(4,1)} %bitcast.67), calls=%async_computation.8 | async-start | bytes 8388608
  427.9 12.1 %copy-start = (f32[2048,1,3,256]{3,0,2,1:T(8,128)S(1)}, f32[2048,1,3,256]{3,0,2,1:T(8,128)}, u32[]{:S(2)}) copy-start(f32[2048,1,3,256]{3,0,2,1:T(8,128)} %copy.55) | copy-start | bytes 18874372
  427.9 12.1 %copy-start.3 = (bf16[2048,768]{0,1:T(8,128)(2,1)S(1)}, bf16[2048,768]{0,1:T(8,128)(2,1)}, u32[]{:S(2)}) copy-start(bf16[2048,768]{0,1:T(8,128)(2,1)} %get-tuple-element.9) | copy-start | bytes 9437188
  427.9 12.1 %copy-start.4 = (f32[3,2,256,256]{3,2,0,1:T(8,128)S(1)}, f32[3,2,256,256]{3,2,0,1:T(8,128)}, u32[]{:S(2)}) copy-start(f32[3,2,256,256]{3,2,0,1:T(8,128)} %bitcast_convert_fusion) | copy-start | bytes 4718596
  446.3 150.9 %reduce-scatter.3.cloned.1.call-start = ((), (), s32[]{:S(2)}) async-start(), calls=%async_computation.3 | async-start | bytes 7864320 | tf_op jit(solution)/shard_map/reduce_scatter | solution.py:74
  463.8 1.9 copy-start.5
  463.8 265.3 %reduce-scatter.5.cloned.1.call-start = ((), (), s32[]{:S(2)}) async-start(), calls=%async_computation.5 | async-start | bytes 14155776 | tf_op jit(solution)/shard_map/reduce_scatter | solution.py:87
Sparse Core Ops, SparseCore 0:
  16.5 83.0 all-gather.4
  101.2 218.2 all-gather.2
  446.4 90.1 all-reduce.1
  539.8 57.3 reduce-scatter.2
  599.9 129.2 reduce-scatter.4
where the time goes:
time: 746 us; the launch traced here: 738 us
  waiting for transfers between devices  429 us (58%)
  matrix products  173 us (23%)
  local copies, waits for them, and re-layouts  77.6 us (10%)
  other arithmetic  44.1 us (6%)
  between operations  14.4 us (2%)
    all_gather x1, waiting for transfers between devices, body(): lax.all_gather(lower_kept, 'row', axis=0, tiled=True)  208 us
    reduce_scatter x1, waiting for transfers between devices, body(): lax.psum_scatter(row_part.reshape(part_cols, supernodes, width), ('row',...  132 us
    dot_general x1, matrix products, body(): lax.dot_general(stacked_inverse, stacked_upper, (((0,), (0,)), ((), ())),...  84 us
    all_gather x1, waiting for transfers between devices, body(): upper_rows = lax.all_gather(upper_kept, 'col', axis=0, tiled=True)  71 us
    dot_general x1, matrix products, body(): jnp.dot(real_inverse, first_part, preferred_element_type=jnp.float32)  35.7 us
    dot_general x1, matrix products, body(): jnp.dot(imag_inverse, second_part, preferred_element_type=jnp.float32)  34.6 us
    unnamed x25, local copies, waits for them, and re-layouts  34.4 us
    reduce_scatter x1, waiting for transfers between devices, body(): lax.psum_scatter(column_part.reshape(part_rows, supernodes, width), ('col...  18.5 us
  transfers between devices with their start and end apart: 5, of which 4 were waited for; matrix products, arithmetic and copies ran while one was open for 21% of the time, Pallas kernels for 0%

commit v1 on v0

v1 whole, which is shorter than its diff:
```python
import functools

import jax
import jax.numpy as jnp
from jax import lax
from jax.experimental import pallas as pl
from jax.experimental.pallas import tpu as pltpu
from jax.sharding import PartitionSpec as P

VMEM_LIMIT = 56 * 1024 * 1024
F32 = jnp.float32
BF16 = jnp.bfloat16


def params(**kw):
    return pltpu.CompilerParams(vmem_limit_bytes=VMEM_LIMIT, **kw)


def cost(flops, nbytes):
    return pl.CostEstimate(flops=int(flops), bytes_accessed=int(nbytes), transcendentals=0)


def whole_vmem():
    return pl.BlockSpec(memory_space=pltpu.VMEM)


def smem():
    return pl.BlockSpec(memory_space=pltpu.SMEM)


def unit_tables(pattern, shards, units, unit_rows, width):
    supers = pattern.shape[0]
    block = (lax.iota(jnp.int32, shards * units) * unit_rows) // width
    hits = jnp.any(pattern[:, :, None] == block[None, None, :], axis=1)
    flags = jnp.transpose(hits).reshape(shards, units * supers).astype(jnp.int32)
    places = lax.iota(jnp.int32, units * supers)
    before = (places[:, None] < places[None, :]).astype(jnp.int32)
    rank = jnp.sum(flags[:, :, None] * before[None], axis=1)
    slot = jnp.where(flags > 0, rank, -1)
    most = jnp.max(jnp.sum(flags, axis=1))
    return slot, most


def pack_kernel(units, supers, unit_rows, transposed, slot_ref, x_ref, *out_refs):
    for u in range(units):
        for s in range(supers):
            slot = slot_ref[u * supers + s]
            for piece in range(supers):

                @pl.when(jnp.logical_and(slot >= piece * units, slot < (piece + 1) * units))
                def _():
                    at = slot - piece * units
                    for h in range(2):
                        tile = x_ref[h, s, u * unit_rows : (u + 1) * unit_rows, :]
                        out_refs[piece][at, h] = tile.T if transposed else tile


def pack(x, slot, units, unit_rows, transposed):
    supers, width = x.shape[1], x.shape[3]
    shape = (units, 2, width, unit_rows) if transposed else (units, 2, unit_rows, width)
    return pl.pallas_call(
        functools.partial(pack_kernel, units, supers, unit_rows, transposed),
        out_shape=[jax.ShapeDtypeStruct(shape, x.dtype)] * supers,
        in_specs=[smem(), whole_vmem()],
        out_specs=[whole_vmem()] * supers,
        compiler_params=params(),
        cost_estimate=cost(0, 4 * x.size),
        name="pack",
    )(slot, x)


def line_gather(x, axis, n):
    hops = []
    right = left = x
    for t in range(1, n):
        right = lax.ppermute(right, axis, [(i, i + 1) for i in range(t - 1, n - 1)])
        left = lax.ppermute(left, axis, [(i + 1, i) for i in range(0, n - t)])
        hops.append((right, left))
    return hops


def pick(shards, d):
    return lax.dynamic_index_in_dim(shards, d, 0, keepdims=False)


def line_scatter(shards, axis, n):
    i = lax.axis_index(axis)
    if n == 1:
        return shards[0]
    if n == 2:
        return pick(shards, i) + lax.ppermute(pick(shards, 1 - i), axis, [(0, 1), (1, 0)])
    right = left = None
    for t in range(n - 1):
        send_right = pick(shards, jnp.clip(n - 1 - t + i, 0, n - 1))
        send_left = pick(shards, jnp.clip(t - (n - 1 - i), 0, n - 1))
        if t:
            send_right, send_left = send_right + right, send_left + left
        right = lax.ppermute(send_right, axis, [(j, j + 1) for j in range(t + 1)])
        left = lax.ppermute(send_left, axis, [(n - 1 - j, n - 2 - j) for j in range(t + 1)])
    return pick(shards, i) + right + left


def direct_sum(x, axes, n):
    i = lax.axis_index(axes)
    parts = x.reshape((n, -1) + x.shape[1:])
    total = pick(parts, i)
    for k in range(1, n):
        ring = [(j, (j + k) % n) for j in range(n)]
        total = total + lax.ppermute(pick(parts, (i + k) % n), axes, ring)
    gathered = [total]
    for k in range(1, n):
        gathered.append(lax.ppermute(total, axes, [((j + k) % n, j) for j in range(n)]))
    stacked = jnp.concatenate([jnp.stack(gathered)] * 2)
    return lax.dynamic_slice_in_dim(stacked, (n - i) % n, n, 0).reshape(x.shape)


def row_kernel(units, supers, sources, width, unit_rows, slot_ref, weight_ref, a_ref, *refs):
    piece_refs = refs[: sources * supers]
    out_ref, left, acc = refs[sources * supers :]
    half = width
    acc[...] = jnp.zeros_like(acc)

    def one(unit, _):
        source = unit // units
        for s in range(supers):
            slot = slot_ref[unit * supers + s]
            for q in range(sources):
                for piece in range(supers):

                    @pl.when(
                        jnp.logical_and(
                            source == q, jnp.logical_and(slot >= piece * units, slot < (piece + 1) * units)
                        )
                    )
                    def _():
                        at = slot - piece * units
                        real = piece_refs[q * supers + piece][at, 0]
                        imag = piece_refs[q * supers + piece][at, 1]
                        left[:half, :unit_rows] = real
                        left[:half, unit_rows:] = -imag
                        left[half:, :unit_rows] = imag
                        left[half:, unit_rows:] = real

            @pl.when(slot >= 0)
            def _():
                rows = pl.ds(pl.multiple_of(unit * unit_rows, unit_rows), unit_rows)
                acc[s] += jnp.dot(left[:, :unit_rows], a_ref[0, rows, :], preferred_element_type=F32) + jnp.dot(
                    left[:, unit_rows:], a_ref[1, rows, :], preferred_element_type=F32
                )

        return 0

    lax.fori_loop(0, sources * units, one, 0)
    for s in range(supers):
        out_ref[0, s * width : (s + 1) * width, :] = -(
            weight_ref[1] * acc[s, :half, :] + weight_ref[0] * acc[s, half:, :]
        )


def row_product(inverse, slot, weights, pieces, units, unit_rows, width, tile):
    supers = len(pieces[0])
    sources = len(pieces)
    part_rows, part_cols = inverse.shape[1:]
    flat = [p for group in pieces for p in group]
    return pl.pallas_call(
        functools.partial(row_kernel, units, supers, sources, width, unit_rows),
        out_shape=jax.ShapeDtypeStruct((part_cols // tile, supers * width, tile), F32),
        grid=(part_cols // tile,),
        in_specs=[smem(), smem(), pl.BlockSpec((2, part_rows, tile), lambda j: (0, 0, j))] + [whole_vmem()] * len(flat),
        out_specs=pl.BlockSpec((1, supers * width, tile), lambda j: (j, 0, 0)),
        scratch_shapes=[pltpu.VMEM((2 * width, 2 * unit_rows), BF16), pltpu.VMEM((supers, 2 * width, tile), F32)],
        compiler_params=params(),
        cost_estimate=cost(4 * supers * part_rows * part_cols * width, 4 * part_rows * part_cols),
        name="row_product",
    )(slot, weights, inverse, *flat)


def column_kernel(cfg, source_ref, slot_ref, *refs):
    units, supers, sources, width, unit_rows, part_rows, first, last, u_sources = cfg
    refs = list(refs)
    weight_ref = refs.pop(0)
    acc_in = None if first else refs.pop(0)
    a_ref = refs.pop(0)
    pieces = [refs.pop(0) for _ in range(sources * supers)]
    u_pieces = [refs.pop(0) for _ in range(u_sources * supers)] if last else []
    if last:
        x_ref, t_ref, acc = refs.pop(0), refs.pop(0), None
    else:
        acc = refs.pop(0)
    right = refs.pop(0)
    if last:
        acc = refs.pop(0)
    step = pl.program_id(0)
    if first:

        @pl.when(step == 0)
        def _():
            acc[...] = jnp.zeros_like(acc)
    else:
        sem = refs.pop(0)

        @pl.when(step == 0)
        def _():
            copy = pltpu.make_async_copy(acc_in, acc, sem)
            copy.start()
            copy.wait()

    source = step // units
    shard = source_ref[source]
    place = shard * units + step % units
    rows_step = min(512, part_rows)

    for s in range(supers):
        slot = jnp.where(shard >= 0, slot_ref[jnp.maximum(place, 0) * supers + s], -1)
        for q in range(sources):
            for piece in range(supers):

                @pl.when(
                    jnp.logical_and(source == q, jnp.logical_and(slot >= piece * units, slot < (piece + 1) * units))
                )
                def _():
                    at = slot - piece * units
                    real = pieces[q * supers + piece][at, 0]
                    imag = pieces[q * supers + piece][at, 1]
                    right[:unit_rows, :width] = real
                    right[:unit_rows, width:] = imag
                    right[unit_rows:, :width] = -imag
                    right[unit_rows:, width:] = real

        @pl.when(slot >= 0)
        def _():
            def tile(m, _):
                rows = pl.ds(pl.multiple_of(m * rows_step, rows_step), rows_step)
                acc[s, rows, :] += jnp.dot(
                    a_ref[0, rows, :], right[:unit_rows, :], preferred_element_type=F32
                ) + jnp.dot(a_ref[1, rows, :], right[unit_rows:, :], preferred_element_type=F32)
                return 0

            lax.fori_loop(0, part_rows // rows_step, tile, 0)

    if last:

        @pl.when(step == sources * units - 1)
        def _():
            weight_real = weight_ref[0]
            weight_imag = weight_ref[1]
            t_ref[...] = jnp.zeros_like(t_ref)

            def chunk(k, _):
                rows = pl.ds(pl.multiple_of(k * unit_rows, unit_rows), unit_rows)
                for s in range(supers):
                    first_acc = acc[s, rows, :width]
                    second_acc = acc[s, rows, width:]
                    mix = weight_imag * first_acc + weight_real * second_acc
                    x_ref[rows, s * width : (s + 1) * width] = -mix
                    slot = slot_ref[slot_base(k) * supers + s]

                    @pl.when(slot >= 0)
                    def _():
                        other = weight_real * first_acc - weight_imag * second_acc
                        stacked = jnp.concatenate([mix, other], axis=0)
                        high = stacked.astype(BF16)
                        low = (stacked - high.astype(F32)).astype(BF16)
                        for q in range(u_sources):
                            for piece in range(supers):

                                @pl.when(
                                    jnp.logical_and(
                                        k // units == q,
                                        jnp.logical_and(slot >= piece * units, slot < (piece + 1) * units),
                                    )
                                )
                                def _():
                                    at = slot - piece * units
                                    real = u_pieces[q * supers + piece][at, 0]
                                    imag = u_pieces[q * supers + piece][at, 1]
                                    both = jnp.concatenate([real, imag], axis=1)
                                    t_ref[s] += jnp.dot(both, high, preferred_element_type=F32) + jnp.dot(
                                        both, low, preferred_element_type=F32
                                    )

                return 0

            def slot_base(k):
                return source_ref[sources] * units + k

            lax.fori_loop(0, part_rows // unit_rows, chunk, 0)


def column_phase(inverse, acc, sources, col_base, u_base, slot, weights, pieces, u_pieces, units, unit_rows, width):
    first = acc is None
    last = u_pieces is not None
    supers = len(pieces[0])
    n_source = len(pieces)
    part_rows, part_cols = inverse.shape[1:]
    u_sources = len(u_pieces) if last else 0
    flat = [p for group in pieces for p in group]
    u_flat = [p for group in u_pieces for p in group] if last else []
    shards = jnp.where(sources >= 0, col_base + sources, -1)
    prefetch = jnp.concatenate([shards, u_base[None], sources]).astype(jnp.int32)
    cfg = (units, supers, n_source, width, unit_rows, part_rows, first, last, u_sources)

    def a_map(g, src, _):
        return (0, 0, jnp.maximum(src[n_source + 1 + g // units], 0) * units + g % units)

    acc_shape = (supers, part_rows, 2 * width)
    in_specs = [smem()] + ([] if first else [pl.BlockSpec(memory_space=pl.ANY)])
    in_specs += [pl.BlockSpec((2, part_rows, unit_rows), a_map)]
    in_specs += [whole_vmem()] * (len(flat) + len(u_flat))
    scratch = [pltpu.VMEM((2 * unit_rows, 2 * width), BF16)]
    if last:
        out_shape = [
            jax.ShapeDtypeStruct((part_rows, supers * width), F32),
            jax.ShapeDtypeStruct((supers, width, width), F32),
        ]
        out_specs = [whole_vmem(), whole_vmem()]
        scratch.append(pltpu.VMEM(acc_shape, F32))
    else:
        out_shape = jax.ShapeDtypeStruct(acc_shape, F32)
        out_specs = whole_vmem()
    if not first:
        scratch.append(pltpu.SemaphoreType.DMA)
    return pl.pallas_call(
        functools.partial(column_kernel, cfg),
        out_shape=out_shape,
        grid_spec=pltpu.PrefetchScalarGridSpec(
            num_scalar_prefetch=2,
            grid=(n_source * units,),
            in_specs=in_specs,
            out_specs=out_specs,
            scratch_shapes=scratch,
        ),
        compiler_params=params(),
        cost_estimate=cost(
            4 * supers * part_rows * units * n_source * unit_rows * width, 4 * part_rows * units * n_source * unit_rows
        ),
        name="column_phase",
    )(prefetch, slot, weights, *([] if first else [acc]), inverse, *flat, *u_flat)


def body(inverse, lower, upper, diag_inverse, weights, pattern):
    n_group = lax.axis_size("groups")
    n_row = lax.axis_size("row")
    n_col = lax.axis_size("col")
    n_pole = lax.axis_size("pole")
    row_index = lax.axis_index("row")
    col_index = lax.axis_index("col")
    local_rows, _, supers, width = lower.shape[1:]
    inverse = inverse[0]
    part_rows, part_cols = inverse.shape[1:]
    unit_rows = min(width, local_rows)
    units = local_rows // unit_rows
    weight = weights[0]

    slot, most = unit_tables(pattern, n_row * n_col, units, unit_rows, width)
    most = most.astype(F32)
    for k in range(1, n_group):
        most = jnp.maximum(most, lax.ppermute(most, "groups", [(j, (j + k) % n_group) for j in range(n_group)]))
    crowded = most > (supers - 1) * units
    flat_slot = slot.reshape(-1)

    lower_parts = jnp.transpose(lower[0], (1, 2, 0, 3))
    own_lower = pack(lower_parts, pick(slot, col_index * n_row + row_index), units, unit_rows, False)
    upper_parts = jnp.transpose(upper[0], (1, 2, 0, 3))
    own_upper = pack(upper_parts, pick(slot, row_index * n_col + col_index), units, unit_rows, True)

    def gather(pieces, axis, n):
        hops = [line_gather(p, axis, n) for p in pieces[:-1]]

        def send(x):
            return line_gather(x, axis, n)

        def skip(x):
            return [(jnp.zeros_like(x), jnp.zeros_like(x)) for _ in range(1, n)]

        hops.append(lax.cond(crowded, send, skip, pieces[-1]))
        return [[[h[t][side] for h in hops] for side in range(2)] for t in range(n - 1)]

    lower_hops = gather(own_lower, "row", n_row)
    upper_hops = gather(own_upper, "col", n_col)

    by_col = []
    for q in range(n_col):
        chosen = own_upper
        for t in range(1, n_col):
            chosen = [
                jnp.where(col_index - t == q, left, jnp.where(col_index + t == q, right, now))
                for now, left, right in zip(chosen, upper_hops[t - 1][0], upper_hops[t - 1][1])
            ]
        by_col.append(chosen)

    upper_base = row_index * n_col
    lower_base = col_index * n_row
    acc = column_phase(
        inverse, None, row_index[None], lower_base, upper_base, flat_slot, weight, [own_lower], None, units, unit_rows, width
    )

    tile = min(512, part_cols)
    row_slot = lax.dynamic_slice_in_dim(slot, upper_base, n_col, 0).reshape(-1)
    row_tiles = row_product(inverse, row_slot, weight, by_col, units, unit_rows, width, tile)

    for t in range(1, n_row):
        low = jnp.where(row_index - t >= 0, row_index - t, -1)
        high = jnp.where(row_index + t < n_row, row_index + t, -1)
        done = t == n_row - 1
        acc = column_phase(
            inverse, acc, jnp.stack([low, high]), lower_base, upper_base, flat_slot, weight, lower_hops[t - 1],
            by_col if done else None, units, unit_rows, width,
        )
    x_part, t_part = acc

    share = part_cols // (n_row * n_pole)
    if share != tile:
        row_tiles = jnp.transpose(row_tiles, (1, 0, 2)).reshape(supers * width, n_row * n_pole, share)
        row_tiles = jnp.transpose(row_tiles, (1, 0, 2))
    row_tiles = row_tiles.reshape(n_row, n_pole, supers * width, share)
    row_sum = line_scatter(jnp.swapaxes(row_tiles, 0, 1), "pole", n_pole)
    row_sum = line_scatter(row_sum, "row", n_row)
    row_density = jnp.transpose(row_sum).reshape(share, supers, width)

    share = part_rows // (n_col * n_pole)
    x_part = jnp.swapaxes(x_part.reshape(n_col, n_pole, share, supers * width), 0, 1)
    col_sum = line_scatter(x_part, "pole", n_pole)
    col_sum = line_scatter(col_sum, "col", n_col)
    column_density = col_sum.reshape(share, supers, width)

    given = diag_inverse[0].astype(F32)
    own_term = weight[0] * given[:, 1] + weight[1] * given[:, 0]
    owner = jnp.logical_and(row_index == 0, col_index == 0)
    t_part = (t_part + jnp.where(owner, own_term, 0.0)).reshape(n_pole, -1, width)
    t_sum = line_scatter(t_part, "pole", n_pole)
    t_sum = direct_sum(t_sum, ("row", "col"), n_row * n_col)
    others = line_gather(t_sum, "pole", n_pole)
    pole_index = lax.axis_index("pole")
    whole = []
    for q in range(n_pole):
        chosen = t_sum
        for t in range(1, n_pole):
            chosen = jnp.where(
                pole_index - t == q, others[t - 1][0], jnp.where(pole_index + t == q, others[t - 1][1], chosen)
            )
        whole.append(chosen)
    diagonal_density = jnp.stack(whole).reshape(supers, width, width)
    return (column_density, row_density, diagonal_density)


def solution(mesh):
    return jax.shard_map(
        body,
        mesh=mesh,
        in_specs=(
            P(("groups", "pole"), None, "row", "col"),
            P(("groups", "pole"), ("col", "row"), None, None, None),
            P(("groups", "pole"), ("row", "col"), None, None, None),
            P(("groups", "pole"), None, None, None, None),
            P(("groups", "pole"), None),
            P("groups", None),
        ),
        out_specs=(
            P(("groups", "row", "col", "pole"), None, None),
            P(("groups", "col", "row", "pole"), None, None),
            P("groups", None, None),
        ),
        check_vma=False,
    )
```

time: 746 us -> 521 us (0.70)
  waiting for transfers between devices: 429 us -> 185 us
  Pallas kernels: 0 us -> 182 us
  matrix products: 173 us -> 0 us
  starting transfers between devices: 0.21 us -> 76.2 us
  local copies, waits for them, and re-layouts: 77.6 us -> 36.7 us
  between operations: 14.4 us -> 2.86 us
  other arithmetic: 44.1 us -> 34.4 us
    all_gather x2 -> x0, waiting for transfers between devices: 279 us -> none  [the longest x1 208 us: body(): lax.all_gather(lower_kept, 'row', axis=0, tiled=True)]
    ppermute x0 -> x43, waiting for transfers between devices: none -> 185 us  [the longest x9 41.6 us: line_gather(): left = lax.ppermute(left, axis, [(i + 1, i) for i in range(0, n - t)])]
    pallas_call x0 -> x7, Pallas kernels: none -> 182 us  [the longest x4 111 us: column_phase(): pl.pallas_call(functools.partial(column_kernel, cfg), out_shape=out_shape...]
    dot_general x5 -> x0, matrix products: 173 us -> none  [the longest x1 84 us: body(): lax.dot_general(stacked_inverse, stacked_upper, (((0,), (0,)), ((), ())),...]
    reduce_scatter x2 -> x0, waiting for transfers between devices: 151 us -> none  [the longest x1 132 us: body(): lax.psum_scatter(row_part.reshape(part_cols, supernodes, width), ('row',...]
    ppermute x0 -> x43, starting transfers between devices: none -> 76.2 us  [the longest x9 26.9 us: line_gather(): right = lax.ppermute(right, axis, [(i, i + 1) for i in range(t - 1, n - 1)])]
    neg x4 -> x0, other arithmetic: 37.6 us -> none  [the longest x1 16.3 us: body(): row_part = -weighted(transposed_terms, weight_real, weight_imag)]
    unnamed x25 -> x56, local copies, waits for them, and re-layouts: 34.4 us -> 11.7 us
  transfers between devices with their start and end apart: 5 -> 43, of which waited for: 4 -> 18; matrix products, arithmetic and copies ran while one was open for 21% -> 8% of each run, Pallas kernels for 0% -> 22%
where the time goes in v1:
time: 521 us; the launch traced here: 517 us
  waiting for transfers between devices  185 us (36%)
  Pallas kernels  182 us (35%)
  starting transfers between devices  76.2 us (15%)
  local copies, waits for them, and re-layouts  36.7 us (7%)
  other arithmetic  34.4 us (7%)
    pallas_call x4, Pallas kernels, column_phase(): pl.pallas_call(functools.partial(column_kernel, cfg), out_shape=out_shape...  111 us
    pallas_call x1, Pallas kernels, row_product(): pl.pallas_call(functools.partial(row_kernel, units, supers, sources, widt...  62.5 us
    ppermute x9, waiting for transfers between devices, line_gather(): left = lax.ppermute(left, axis, [(i + 1, i) for i in range(0, n - t)])  41.6 us
    ppermute x7, waiting for transfers between devices, direct_sum(): lax.ppermute(total, axes, [((j + k) % n, j) for j in range(n)])  37.1 us
    ppermute x7, waiting for transfers between devices, direct_sum(): total = total + lax.ppermute(pick(parts, (i + k) % n), axes, ring)  30.6 us
    ppermute x3, waiting for transfers between devices, line_scatter(): lax.ppermute(send_left, axis, [(n - 1 - j, n - 2 - j) for j in range(t +...  29 us
    ppermute x9, waiting for transfers between devices, line_gather(): right = lax.ppermute(right, axis, [(i, i + 1) for i in range(t - 1, n - 1)])  28.8 us
    ppermute x9, starting transfers between devices, line_gather(): right = lax.ppermute(right, axis, [(i, i + 1) for i in range(t - 1, n - 1)])  26.9 us
  transfers between devices with their start and end apart: 43, of which 18 were waited for; matrix products, arithmetic and copies ran while one was open for 8% of the time, Pallas kernels for 22%

profile of v1, /device:TPU:0, one launch (start us, length us, event | category | flops | bytes accessed | tf_op | source)
XLA Modules:
  0.0 516.8 jit_solution(15291975288905334287)
XLA Ops:
  10.6 5.2 %collective-permute-start.23 = (bf16[4,2,256,256]{3,2,1,0:T(8,128)(2,1)}, bf16[4,2,256,256]{3,2,1,0:T(8,128)(2,1)S(1)}, u32[]{:S(2)}, u32[]{:S(2)}) collective-permute-start(bf16[4,2,256,256]{3,2,1,0:T(8,128)(2,1)} %get-tuple-element.31), channel_id=1, source_target_pairs={{0,2},{1,3},{4,6},{5,7},{8,10},{9,11},{12,14},{13,15},{16,18},{17,... | collective-permute-start | bytes 3145736 | tf_op jit(solution)/shard_map/ppermute | solution.py:76
  21.3 5.6 %collective-permute-start.21 = (bf16[4,2,256,256]{3,2,1,0:T(8,128)(2,1)}, bf16[4,2,256,256]{3,2,1,0:T(8,128)(2,1)}, u32[]{:S(2)}, u32[]{:S(2)}) collective-permute-start(bf16[4,2,256,256]{3,2,1,0:T(8,128)(2,1)} %get-tuple-element.30), channel_id=1, source_target_pairs={{0,2},{1,3},{4,6},{5,7},{8,10},{9,11},{12,14},{13,15},{16,18},{17,... | collective-permute-start | bytes 3145736 | tf_op jit(solution)/shard_map/ppermute | solution.py:76
  45.6 15.4 %collective-permute-done.21 = bf16[4,2,256,256]{3,2,1,0:T(8,128)(2,1)} collective-permute-done((bf16[4,2,256,256]{3,2,1,0:T(8,128)(2,1)}, bf16[4,2,256,256]{3,2,1,0:T(8,128)(2,1)}, u32[]{:S(2)}, u32[]{:S(2)}) %collective-permute-start.21) | collective-permute-done | bytes 1048608 | tf_op jit(solution)/shard_map/ppermute | solution.py:76
  68.3 62.5 %row_product.1 = f32[8,768,512]{2,1,0:T(8,128)} custom-call(s32[24]{0:T(128)} %reshape.105.slot_ref, f32[2]{0:T(128)} %bitcast.165, bf16[2,2048,4096]{2,1,0:T(8,128)(2,1)} %bitcast.143, bf16[4,2,256,256]{3,2,1,0:T(8,128)(2,1)} %get-tuple-element.60.refs_9_.refs_0_, bf16[4,2,256,256]{3,2,1,0:T(8,128)(2,1)} %get-tuple-element.58.refs_10_.refs_1_, ...), custom_call_target="tpu_custom_call" | custom-call | flops 25769803776 | bytes 33554432 | tf_op jit(solution)/shard_map/row_product/pallas_call | solution.py:165
  130.7 6.3 %dynamic-slice_bitcast_fusion = f32[4,768,512]{2,1,0:T(8,128)} fusion(f32[4,2,768,512]{3,2,1,0:T(8,128)} %bitcast.150, s32[]{:T(128)S(6)} %select_n.277), kind=kLoop, calls=%fused_computation.1 | loop fusion | bytes 12582916 | tf_op jit(solution)/shard_map/jit(dynamic_index_in_dim)/squeeze | solution.py:83
  143.9 4.6 collective-permute-start.8
  148.6 6.4 %conditional.2 = (bf16[4,2,256,256]{3,2,1,0:T(8,128)(2,1)}, bf16[4,2,256,256]{3,2,1,0:T(8,128)(2,1)}, bf16[4,2,256,256]{3,2,1,0:T(8,128)(2,1)}, bf16[4,2,256,256...) conditional(s32[]{:T(128)} %convert_element_type.46, () %tuple.24, ...), branch_computations={%region_5.6_spmd, %region_6.7_spmd} | conditional | bytes 25166112 | solution.py:376
  156.2 5.6 %collective-permute-start.9 = (bf16[4,2,256,256]{3,2,1,0:T(8,128)(2,1)}, bf16[4,2,256,256]{3,2,1,0:T(8,128)(2,1)}, u32[]{:S(2)}, u32[]{:S(2)}) collective-permute-start(bf16[4,2,256,256]{3,2,1,0:T(8,128)(2,1)} %get-tuple-element.22.refs_3_), channel_id=1, source_target_pairs={{0,4},{4,8},{8,12},{1,5},{5,9},{9,13},{2,6},{6,10},{10,14},{3,7},{... | collective-permute-start | bytes 3145736 | tf_op jit(solution)/shard_map/ppermute | solution.py:76
  166.7 17.7 %column_phase.4.refs_1_ = f32[3,2048,512]{2,1,0:T(8,128)} custom-call(s32[3]{0:T(128)} %pad_add_fusion.6.source_ref, s32[96]{0:T(128)} %broadcast_select_fusion.slot_ref, f32[2]{0:T(128)} %bitcast.166, bf16[2,2048,4096]{2,1,0:T(8,128)(2,1)} %bitcast.144, bf16[4,2,256,256]{3,2,1,0:T(8,128)(2,1)} %get-tuple-element.21.refs_2_, ...), custom_call_target="tpu_custom_call" | custom-call | flops 6442450944 | bytes 8388608 | tf_op jit(solution)/shard_map/column_phase/pallas_call | solution.py:323
  185.2 8.9 %collective-permute-done.9.refs_4_ = bf16[4,2,256,256]{3,2,1,0:T(8,128)(2,1)} collective-permute-done((bf16[4,2,256,256]{3,2,1,0:T(8,128)(2,1)}, bf16[4,2,256,256]{3,2,1,0:T(8,128)(2,1)}, u32[]{:S(2)}, u32[]{:S(2)}) %collective-permute-start.9) | collective-permute-done | bytes 1048608 | tf_op jit(solution)/shard_map/ppermute | solution.py:76
  197.5 30.2 %column_phase.5.refs_1_ = f32[3,2048,512]{2,1,0:T(8,128)} custom-call(s32[5]{0:T(128)} %pad_add_fusion.5.source_ref, s32[96]{0:T(128)} %broadcast_select_fusion.slot_ref, f32[2]{0:T(128)} %bitcast.167, f32[3,2048,512]{2,1,0:T(8,128)} %column_phase.4.refs_1_, bf16[2,2048,4096]{2,1,0:T(8,128)(2,1)} %bitcast.145, bf16[4,2,256,256]{3,2,1,0:T(8,128)(2,1)} %copy-done.4, ...), custom_call_target="tpu_custom_call" | custom-call | flops 12884901888 | bytes 16777216 | tf_op jit(solution)/shard_map/column_phase/pallas_call | solution.py:323
  231.4 17.8 %collective-permute-done.16.refs_7_ = bf16[4,2,256,256]{3,2,1,0:T(8,128)(2,1)} collective-permute-done((bf16[4,2,256,256]{3,2,1,0:T(8,128)(2,1)S(1)}, bf16[4,2,256,256]{3,2,1,0:T(8,128)(2,1)}, u32[]{:S(2)}, u32[]{:S(2)}) %collective-permute-start.16) | collective-permute-done | bytes 1048608 | tf_op jit(solution)/shard_map/ppermute | solution.py:77
  250.6 28.4 %column_phase.6.refs_1_ = f32[3,2048,512]{2,1,0:T(8,128)} custom-call(s32[5]{0:T(128)} %get-tuple-element.77.source_ref, s32[96]{0:T(128)} %broadcast_select_fusion.slot_ref, f32[2]{0:T(128)} %bitcast.168, f32[3,2048,512]{2,1,0:T(8,128)} %column_phase.5.refs_1_, bf16[2,2048,4096]{2,1,0:T(8,128)(2,1)} %bitcast.146, bf16[4,2,256,256]{3,2,1,0:T(8,128)(2,1)} %copy-done.6, ...), custom_call_target="tpu_custom_call" | custom-call | flops 12884901888 | bytes 16777216 | tf_op jit(solution)/shard_map/column_phase/pallas_call | solution.py:323
  279.1 12.7 %collective-permute-done.20.refs_7_ = bf16[4,2,256,256]{3,2,1,0:T(8,128)(2,1)S(1)} collective-permute-done((bf16[4,2,256,256]{3,2,1,0:T(8,128)(2,1)}, bf16[4,2,256,256]{3,2,1,0:T(8,128)(2,1)S(1)}, u32[]{:S(2)}, u32[]{:S(2)}) %collective-permute-start.20) | collective-permute-done | bytes 1048608 | tf_op jit(solution)/shard_map/ppermute | solution.py:77
  292.8 35.1 %column_phase.7 = (f32[2048,768]{1,0:T(8,128)}, f32[3,256,256]{2,1,0:T(8,128)}) custom-call(s32[5]{0:T(128)} %get-tuple-element.76.source_ref, s32[96]{0:T(128)} %broadcast_select_fusion.slot_ref, f32[2]{0:T(128)} %bitcast.169, f32[3,2048,512]{2,1,0:T(8,128)} %column_phase.6.refs_1_, bf16[2,2048,4096]{2,1,0:T(8,128)(2,1)} %bitcast.147, ...), custom_call_target="tpu_custom_call" | custom-call | flops 12884901888 | bytes 16777216 | tf_op jit(solution)/shard_map/column_phase/pallas_call | solution.py:323
  330.4 6.2 %bitcast_add_fusion = f32[4,768,512]{2,1,0:T(8,128)S(1)} fusion(f32[4,768,512]{2,1,0:T(8,128)} %collective-permute-done.27, f32[4,2,768,512]{3,2,1,0:T(8,128)} %bitcast.151, s32[]{:T(128)S(6)} %select_n.276), kind=kLoop, calls=%fused_computation | loop fusion | flops 1572864 | bytes 18874372 | tf_op jit(solution)/shard_map/add | solution.py:91
  343.8 5.0 collective-permute-start.38
  350.9 26.2 %collective-permute-done.36 = f32[48,256]{1,0:T(8,128)S(1)} collective-permute-done((f32[48,256]{1,0:T(8,128)S(1)}, f32[48,256]{1,0:T(8,128)S(1)}, u32[]{:S(2)}, u32[]{:S(2)}) %collective-permute-start.36) | collective-permute-done | bytes 49184 | tf_op jit(solution)/shard_map/ppermute | solution.py:109
  377.7 4.6 collective-permute-start.41
  384.2 5.1 collective-permute-start.42
  400.6 31.9 %collective-permute-done.46 = f32[48,256]{1,0:T(8,128)S(1)} collective-permute-done((f32[48,256]{1,0:T(8,128)S(1)}, f32[48,256]{1,0:T(8,128)S(1)}, u32[]{:S(2)}, u32[]{:S(2)}) %collective-permute-start.46) | collective-permute-done | bytes 49184 | tf_op jit(solution)/shard_map/ppermute | solution.py:112
  444.4 5.8 %collective-permute-start.30 = (f32[768,512]{1,0:T(8,128)}, f32[768,512]{1,0:T(8,128)}, u32[]{:S(2)}, u32[]{:S(2)}) collective-permute-start(f32[768,512]{1,0:T(8,128)} %get-tuple-element.51), channel_id=1, source_target_pairs={{0,4},{4,8},{8,12},{1,5},{5,9},{9,13},{2,6},{6,10},{10,14},{3,7},{... | collective-permute-start | bytes 4718600 | tf_op jit(solution)/shard_map/ppermute | solution.py:98
  460.9 16.1 %collective-permute-done.26 = f32[512,768]{1,0:T(8,128)} collective-permute-done((f32[512,768]{1,0:T(8,128)}, f32[512,768]{1,0:T(8,128)}, u32[]{:S(2)}, u32[]{:S(2)}) %collective-permute-start.26) | collective-permute-done | bytes 1572896 | tf_op jit(solution)/shard_map/ppermute | solution.py:91
  483.3 29.0 %collective-permute-done.33 = f32[768,512]{1,0:T(8,128)} collective-permute-done((f32[768,512]{1,0:T(8,128)}, f32[768,512]{1,0:T(8,128)}, u32[]{:S(2)}, u32[]{:S(2)}) %collective-permute-start.33) | collective-permute-done | bytes 1572896 | tf_op jit(solution)/shard_map/ppermute | solution.py:99
  (188 shorter events, 129.9 us)
Async XLA Ops:
  21.3 39.6 %collective-permute-start.21 = (bf16[4,2,256,256]{3,2,1,0:T(8,128)(2,1)}, bf16[4,2,256,256]{3,2,1,0:T(8,128)(2,1)}, u32[]{:S(2)}, u32[]{:S(2)}) collective-permute-start(bf16[4,2,256,256]{3,2,1,0:T(8,128)(2,1)} %get-tuple-element.30), channel_id=1, source_target_pairs={{0,2},{1,3},{4,6},{5,7},{8,10},{9,11},{12,14},{13,15},{16,18},{17,... | collective-permute-start | bytes 3145736 | tf_op jit(solution)/shard_map/ppermute | solution.py:76
  29.7 35.4 %collective-permute-start.22 = (bf16[4,2,256,256]{3,2,1,0:T(8,128)(2,1)S(1)}, bf16[4,2,256,256]{3,2,1,0:T(8,128)(2,1)}, u32[]{:S(2)}, u32[]{:S(2)}) collective-permute-start(bf16[4,2,256,256]{3,2,1,0:T(8,128)(2,1)S(1)} %copy-done.14), channel_id=1, source_target_pairs={{2,0},{3,1},{6,4},{7,5},{10,8},{11,9},{14,12},{15,13},{18,16},{19,... | collective-permute-start | bytes 3145736 | tf_op jit(solution)/shard_map/ppermute | solution.py:77
  137.1 193.4 %collective-permute-start.27 = (f32[4,768,512]{2,1,0:T(8,128)}, f32[4,768,512]{2,1,0:T(8,128)}, u32[]{:S(2)}, u32[]{:S(2)}) collective-permute-start(f32[4,768,512]{2,1,0:T(8,128)} %dynamic-slice_bitcast_fusion), channel_id=1, source_target_pairs={{0,1},{1,0},{2,3},{3,2},{4,5},{5,4},{6,7},{7,6},{8,9},{9,8},{10,11... | collective-permute-start | bytes 18874376 | tf_op jit(solution)/shard_map/ppermute | solution.py:91
  142.6 52.1 %collective-permute-start.11 = (bf16[4,2,256,256]{3,2,1,0:T(8,128)(2,1)}, bf16[4,2,256,256]{3,2,1,0:T(8,128)(2,1)S(1)}, u32[]{:S(2)}, u32[]{:S(2)}) collective-permute-start(bf16[4,2,256,256]{3,2,1,0:T(8,128)(2,1)} %get-tuple-element.21.refs_2_), channel_id=1, source_target_pairs={{4,0},{8,4},{12,8},{5,1},{9,5},{13,9},{6,2},{10,6},{14,10},{7,3},{... | collective-permute-start | bytes 3145736 | tf_op jit(solution)/shard_map/ppermute | solution.py:77
  143.9 40.5 %collective-permute-start.8 = (bf16[4,2,256,256]{3,2,1,0:T(8,128)(2,1)}, bf16[4,2,256,256]{3,2,1,0:T(8,128)(2,1)S(1)}, u32[]{:S(2)}, u32[]{:S(2)}) collective-permute-start(bf16[4,2,256,256]{3,2,1,0:T(8,128)(2,1)} %get-tuple-element.21.refs_2_), channel_id=1, source_target_pairs={{0,4},{4,8},{8,12},{1,5},{5,9},{9,13},{2,6},{6,10},{10,14},{3,7},{... | collective-permute-start | bytes 3145736 | tf_op jit(solution)/shard_map/ppermute | solution.py:76
  155.0 41.1 %collective-permute-start.12 = (bf16[4,2,256,256]{3,2,1,0:T(8,128)(2,1)}, bf16[4,2,256,256]{3,2,1,0:T(8,128)(2,1)S(1)}, u32[]{:S(2)}, u32[]{:S(2)}) collective-permute-start(bf16[4,2,256,256]{3,2,1,0:T(8,128)(2,1)} %get-tuple-element.22.refs_3_), channel_id=1, source_target_pairs={{4,0},{8,4},{12,8},{5,1},{9,5},{13,9},{6,2},{10,6},{14,10},{7,3},{... | collective-permute-start | bytes 3145736 | tf_op jit(solution)/shard_map/ppermute | solution.py:77
  156.2 37.8 %collective-permute-start.9 = (bf16[4,2,256,256]{3,2,1,0:T(8,128)(2,1)}, bf16[4,2,256,256]{3,2,1,0:T(8,128)(2,1)}, u32[]{:S(2)}, u32[]{:S(2)}) collective-permute-start(bf16[4,2,256,256]{3,2,1,0:T(8,128)(2,1)} %get-tuple-element.22.refs_3_), channel_id=1, source_target_pairs={{0,4},{4,8},{8,12},{1,5},{5,9},{9,13},{2,6},{6,10},{10,14},{3,7},{... | collective-permute-start | bytes 3145736 | tf_op jit(solution)/shard_map/ppermute | solution.py:76
  184.4 43.2 %collective-permute-start.13 = (bf16[4,2,256,256]{3,2,1,0:T(8,128)(2,1)S(1)}, bf16[4,2,256,256]{3,2,1,0:T(8,128)(2,1)S(1)}, u32[]{:S(2)}, u32[]{:S(2)}) collective-permute-start(bf16[4,2,256,256]{3,2,1,0:T(8,128)(2,1)S(1)} %collective-permute-done.8.refs_3_), channel_id=1, source_target_pairs={{4,8},{8,12},{5,9},{9,13},{6,10},{10,14},{7,11},{11,15},{20,24},{2... | collective-permute-start | bytes 3145736 | tf_op jit(solution)/shard_map/ppermute | solution.py:76
  194.1 34.4 %collective-permute-start.14 = (bf16[4,2,256,256]{3,2,1,0:T(8,128)(2,1)}, bf16[4,2,256,256]{3,2,1,0:T(8,128)(2,1)S(1)}, u32[]{:S(2)}, u32[]{:S(2)}) collective-permute-start(bf16[4,2,256,256]{3,2,1,0:T(8,128)(2,1)} %collective-permute-done.9.refs_4_), channel_id=1, source_target_pairs={{4,8},{8,12},{5,9},{9,13},{6,10},{10,14},{7,11},{11,15},{20,24},{2... | collective-permute-start | bytes 3145736 | tf_op jit(solution)/shard_map/ppermute | solution.py:76
  194.8 35.3 %collective-permute-start.15 = (bf16[4,2,256,256]{3,2,1,0:T(8,128)(2,1)S(1)}, bf16[4,2,256,256]{3,2,1,0:T(8,128)(2,1)S(1)}, u32[]{:S(2)}, u32[]{:S(2)}) collective-permute-start(bf16[4,2,256,256]{3,2,1,0:T(8,128)(2,1)S(1)} %collective-permute-done.11.refs_6_), channel_id=1, source_target_pairs={{4,0},{8,4},{5,1},{9,5},{6,2},{10,6},{7,3},{11,7},{20,16},{24,20},... | collective-permute-start | bytes 3145736 | tf_op jit(solution)/shard_map/ppermute | solution.py:77
  196.1 53.1 %collective-permute-start.16 = (bf16[4,2,256,256]{3,2,1,0:T(8,128)(2,1)S(1)}, bf16[4,2,256,256]{3,2,1,0:T(8,128)(2,1)}, u32[]{:S(2)}, u32[]{:S(2)}) collective-permute-start(bf16[4,2,256,256]{3,2,1,0:T(8,128)(2,1)S(1)} %collective-permute-done.12.refs_7_), channel_id=1, source_target_pairs={{4,0},{8,4},{5,1},{9,5},{6,2},{10,6},{7,3},{11,7},{20,16},{24,20},... | collective-permute-start | bytes 3145736 | tf_op jit(solution)/shard_map/ppermute | solution.py:77
  227.7 51.3 %collective-permute-start.17 = (bf16[4,2,256,256]{3,2,1,0:T(8,128)(2,1)S(1)}, bf16[4,2,256,256]{3,2,1,0:T(8,128)(2,1)S(1)}, u32[]{:S(2)}, u32[]{:S(2)}) collective-permute-start(bf16[4,2,256,256]{3,2,1,0:T(8,128)(2,1)S(1)} %collective-permute-done.13.refs_3_), channel_id=1, source_target_pairs={{8,12},{9,13},{10,14},{11,15},{24,28},{25,29},{26,30},{27,31}} | collective-permute-start | bytes 3145736 | tf_op jit(solution)/shard_map/ppermute | solution.py:76
  228.5 50.6 %collective-permute-start.18 = (bf16[4,2,256,256]{3,2,1,0:T(8,128)(2,1)S(1)}, bf16[4,2,256,256]{3,2,1,0:T(8,128)(2,1)}, u32[]{:S(2)}, u32[]{:S(2)}) collective-permute-start(bf16[4,2,256,256]{3,2,1,0:T(8,128)(2,1)S(1)} %collective-permute-done.14.refs_4_), channel_id=1, source_target_pairs={{8,12},{9,13},{10,14},{11,15},{24,28},{25,29},{26,30},{27,31}} | collective-permute-start | bytes 3145736 | tf_op jit(solution)/shard_map/ppermute | solution.py:76
  230.1 48.9 %collective-permute-start.19 = (bf16[4,2,256,256]{3,2,1,0:T(8,128)(2,1)S(1)}, bf16[4,2,256,256]{3,2,1,0:T(8,128)(2,1)S(1)}, u32[]{:S(2)}, u32[]{:S(2)}) collective-permute-start(bf16[4,2,256,256]{3,2,1,0:T(8,128)(2,1)S(1)} %collective-permute-done.15.refs_6_), channel_id=1, source_target_pairs={{4,0},{5,1},{6,2},{7,3},{20,16},{21,17},{22,18},{23,19}} | collective-permute-start | bytes 3145736 | tf_op jit(solution)/shard_map/ppermute | solution.py:77
  249.3 42.5 %collective-permute-start.20 = (bf16[4,2,256,256]{3,2,1,0:T(8,128)(2,1)}, bf16[4,2,256,256]{3,2,1,0:T(8,128)(2,1)S(1)}, u32[]{:S(2)}, u32[]{:S(2)}) collective-permute-start(bf16[4,2,256,256]{3,2,1,0:T(8,128)(2,1)} %collective-permute-done.16.refs_7_), channel_id=1, source_target_pairs={{4,0},{5,1},{6,2},{7,3},{20,16},{21,17},{22,18},{23,19}} | collective-permute-start | bytes 3145736 | tf_op jit(solution)/shard_map/ppermute | solution.py:77
  340.2 54.4 %collective-permute-start.28 = (f32[768,512]{1,0:T(8,128)}, f32[768,512]{1,0:T(8,128)S(1)}, u32[]{:S(2)}, u32[]{:S(2)}) collective-permute-start(f32[768,512]{1,0:T(8,128)} %get-tuple-element.53), channel_id=1, source_target_pairs={{0,4},{1,5},{2,6},{3,7},{16,20},{17,21},{18,22},{19,23}} | collective-permute-start | bytes 4718600 | tf_op jit(solution)/shard_map/ppermute | solution.py:98
  343.6 34.1 %collective-permute-start.37 = (f32[48,256]{1,0:T(8,128)S(1)}, f32[48,256]{1,0:T(8,128)S(1)}, u32[]{:S(2)}, u32[]{:S(2)}) collective-permute-start(f32[48,256]{1,0:T(8,128)S(1)} %get-tuple-element.68), channel_id=1, source_target_pairs={{0,6},{2,8},{4,10},{6,12},{8,14},{10,0},{12,2},{14,4},{1,7},{3,9},... | collective-permute-start | bytes 147464 | tf_op jit(solution)/shard_map/ppermute | solution.py:109
  343.8 38.6 %collective-permute-start.38 = (f32[48,256]{1,0:T(8,128)S(1)}, f32[48,256]{1,0:T(8,128)S(1)}, u32[]{:S(2)}, u32[]{:S(2)}) collective-permute-start(f32[48,256]{1,0:T(8,128)S(1)} %get-tuple-element.67), channel_id=1, source_target_pairs={{0,8},{2,10},{4,12},{6,14},{8,0},{10,2},{12,4},{14,6},{1,9},{3,11}... | collective-permute-start | bytes 147464 | tf_op jit(solution)/shard_map/ppermute | solution.py:109
  391.5 50.8 %collective-permute-start.25 = (f32[2,512,768]{2,1,0:T(8,128)S(1)}, f32[2,512,768]{2,1,0:T(8,128)S(1)}, u32[]{:S(2)}, u32[]{:S(2)}) collective-permute-start(f32[2,512,768]{2,1,0:T(8,128)S(1)} %dynamic-slice_bitcast_fusion.1), channel_id=1, source_target_pairs={{0,1},{1,0},{2,3},{3,2},{4,5},{5,4},{6,7},{7,6},{8,9},{9,8},{10,11... | collective-permute-start | bytes 9437192 | tf_op jit(solution)/shard_map/ppermute | solution.py:91
  394.6 44.8 %collective-permute-start.31 = (f32[768,512]{1,0:T(8,128)}, f32[768,512]{1,0:T(8,128)S(1)}, u32[]{:S(2)}, u32[]{:S(2)}) collective-permute-start(f32[768,512]{1,0:T(8,128)} %get-tuple-element.54), channel_id=1, source_target_pairs={{12,8},{13,9},{14,10},{15,11},{28,24},{29,25},{30,26},{31,27}} | collective-permute-start | bytes 4718600 | tf_op jit(solution)/shard_map/ppermute | solution.py:99
  397.2 42.2 %collective-permute-start.29 = (f32[768,512]{1,0:T(8,128)S(1)}, f32[768,512]{1,0:T(8,128)S(1)}, u32[]{:S(2)}, u32[]{:S(2)}) collective-permute-start(f32[768,512]{1,0:T(8,128)S(1)} %bitcast_add_fusion.4), channel_id=1, source_target_pairs={{0,4},{4,8},{1,5},{5,9},{2,6},{6,10},{3,7},{7,11},{16,20},{20,24},... | collective-permute-start | bytes 4718600 | tf_op jit(solution)/shard_map/ppermute | solution.py:98
  400.6 35.1 %collective-permute-start.47 = (f32[48,256]{1,0:T(8,128)S(1)}, f32[48,256]{1,0:T(8,128)S(1)}, u32[]{:S(2)}, u32[]{:S(2)}) collective-permute-start(f32[48,256]{1,0:T(8,128)S(1)} %get-tuple-element.50), channel_id=1, source_target_pairs={{12,0},{14,2},{0,4},{2,6},{4,8},{6,10},{8,12},{10,14},{13,1},{15,3... | collective-permute-start | bytes 147464 | tf_op jit(solution)/shard_map/ppermute | solution.py:112
  444.4 38.9 %collective-permute-start.30 = (f32[768,512]{1,0:T(8,128)}, f32[768,512]{1,0:T(8,128)}, u32[]{:S(2)}, u32[]{:S(2)}) collective-permute-start(f32[768,512]{1,0:T(8,128)} %get-tuple-element.51), channel_id=1, source_target_pairs={{0,4},{4,8},{8,12},{1,5},{5,9},{9,13},{2,6},{6,10},{10,14},{3,7},{... | collective-permute-start | bytes 4718600 | tf_op jit(solution)/shard_map/ppermute | solution.py:98
  451.7 60.7 %collective-permute-start.33 = (f32[768,512]{1,0:T(8,128)}, f32[768,512]{1,0:T(8,128)}, u32[]{:S(2)}, u32[]{:S(2)}) collective-permute-start(f32[768,512]{1,0:T(8,128)} %bitcast_add_fusion.3), channel_id=1, source_target_pairs={{12,8},{8,4},{4,0},{13,9},{9,5},{5,1},{14,10},{10,6},{6,2},{15,11}... | collective-permute-start | bytes 4718600 | tf_op jit(solution)/shard_map/ppermute | solution.py:99
  (38 other events, 500.4 us)
